TPU v7x, 32 devices: a whole 2x2x4 slice. The times are simulated.
32 devices in a mesh: aux: 16 (over z, x, core), pair: 2 (over y).
Axes of the slice: x: 2, y: 2, z: 4, core: 2. Of those that a mesh axis runs over, the one named last changes fastest.
Arguments:
- blocks: bfloat16 [16, 2, 32, 128, 128], P('aux', 'pair'), may hold values from -6 to 6
- block_list: int32 [16, 2, 32, 3], P('aux', 'pair'), may hold values from -1 to 79, as said below
- metric: bfloat16 [4096, 256], P('aux'), may hold values from -0.1875 to 0.1875
- virt_energy: float32 [20480], replicated, may hold values from 0.2 to 3
- occ_energy: float32 [8000], replicated, may hold values from -2 to -0.5
- pair_list: int32 [1, 2], replicated, may hold values from 0 to 7999
Outputs:
- amplitudes: bfloat16 [2, 16, 10240], P('pair', None, 'aux')
- density: float32 [8, 8], replicated
Inputs may be any that keep to these rules, and one draw needn't show every extreme that they name: `block_list`: each entry is (occupied slot, virtual block, auxiliary block). Live entries have slot 0 or 1 (the pair's first or second orbital), virtual block 0 to 79 within the device's virtual half, auxiliary block 0 or 1; padding entries have slot -1 and stand anywhere in the list; no live triple repeats within one device's list; in every draw some device has all 32 entries live and some device has padding.
All inputs are finite; a program needn't handle non-finite values.
Results may differ from a plain program's by a relative error of at most 0.0049.
Values may be sent and summed in bfloat16 or wider, within the bound.
A program may use at most 128 MiB of HBM per device.

v0:
```python
import math

import jax
import jax.numpy as jnp
from jax import lax
from jax.sharding import PartitionSpec as P

V = 20480
HALF = 8


def partner(value, axis, bit):
    mask = 2**bit
    pairs = [(source, source ^ mask) for source in range(lax.axis_size(axis))]
    return lax.ppermute(value, axis, pairs)


def body(blocks, block_list, metric, virt_energy, occ_energy, pair_list):
    raw_blocks = blocks[0, 0]
    entries = block_list[0, 0]
    block_rows = raw_blocks.shape[1]
    block_aux = raw_blocks.shape[2]
    shard_aux = metric.shape[1]
    half_width = V // 2
    aux_count = lax.axis_size("aux")
    slab_rows = half_width // aux_count
    vblock_count = half_width // block_rows
    metric_pair = metric.reshape(2, block_aux, shard_aux)
    occ_slot = entries[:, 0]
    aux_block = entries[:, 2]
    slot_index = jnp.where(occ_slot >= 0, occ_slot * vblock_count + entries[:, 1], 2 * vblock_count)
    picked = jnp.where((aux_block == 0)[:, None, None], metric_pair[0][None], metric_pair[1][None])
    terms = jnp.einsum("evk,ekn->evn", raw_blocks, picked, preferred_element_type=jnp.float32)
    summed = jax.ops.segment_sum(terms, slot_index, num_segments=2 * vblock_count)
    local_rows = summed.astype(jnp.bfloat16).reshape(2, half_width, shard_aux)
    pair_position = lax.axis_index("pair")
    half_index = pair_position % 2
    own_rows = local_rows[:, :HALF, :]
    partner_rows = partner(own_rows, "pair", 0)
    window_rows = jnp.where(
        half_index == 0,
        jnp.concatenate([own_rows, partner_rows], axis=1),
        jnp.concatenate([partner_rows, own_rows], axis=1),
    )
    regrouped = lax.all_to_all(local_rows, "aux", split_axis=1, concat_axis=2, tiled=True)
    coulomb = jnp.einsum(
        "owk,osk->ows",
        lax.all_gather(window_rows, "aux", axis=2, tiled=True),
        regrouped[::-1],
        preferred_element_type=jnp.float32,
    )
    window_energy = jnp.concatenate(
        [virt_energy[:HALF], virt_energy[half_width : half_width + HALF]]
    )
    slab_start = half_index * half_width + lax.axis_index("aux") * slab_rows
    slab_energy = lax.dynamic_slice_in_dim(virt_energy, slab_start, slab_rows)
    pair_row = lax.dynamic_index_in_dim(pair_list, pair_position // 2, 0, keepdims=False)
    first_energy = lax.dynamic_index_in_dim(occ_energy, pair_row[0], 0, keepdims=False)
    second_energy = lax.dynamic_index_in_dim(occ_energy, pair_row[1], 0, keepdims=False)
    denominator = window_energy[:, None] + slab_energy[None, :] - first_energy - second_energy
    scaled = (coulomb / denominator[None]).astype(jnp.bfloat16)
    head_rows = scaled[:, :HALF]
    tail_rows = scaled[:, HALF:]
    gram = jnp.einsum("oac,pbc->oapb", head_rows, tail_rows, preferred_element_type=jnp.float32)
    partial_density = 2.0 * (gram[0, :, 0] + gram[1, :, 1]) - gram[1, :, 0] - gram[0, :, 1]
    density = lax.psum(partial_density, ("aux", "pair")) / math.sqrt(V)
    return (scaled[0][None], density)


def solution(mesh):
    in_specs = (
        P("aux", "pair", None, None, None),
        P("aux", "pair", None, None),
        P("aux", None),
        P(),
        P(),
        P(),
    )
    out_specs = (P("pair", None, "aux"), P())
    return jax.shard_map(body, mesh=mesh, in_specs=in_specs, out_specs=out_specs, check_vma=False)
```

profile of v0, /device:TPU:0, one launch (start us, length us, event | category | flops | bytes accessed | tf_op | source)
XLA Modules:
  0.0 433.0 jit_solution(14121879211524464913)
XLA Ops:
  0.6 0.0 copy-start
  0.6 0.8 copy.20
  1.4 0.9 fusion.10
  2.3 0.1 copy.13
  2.4 0.1 copy.12
  2.6 0.0 copy-done
  2.6 2.7 convolution_bitcast_fusion
  5.3 5.6 %copy.14 = f32[32,128,256]{2,1,0:T(8,128)} copy(f32[32,128,256]{1,2,0:T(8,128)} %convolution_bitcast_fusion) | data formatting | bytes 8388608 | tf_op jit(solution)/shard_map/evk,ekn->evn/dot_general | solution.py:33
  10.9 9.6 %broadcast_in_dim.36 = f32[160,128,256]{2,1,0:T(8,128)} broadcast(f32[]{:T(128)} %constant.49.clone.1), dimensions={} | broadcast | bytes 20971524 | tf_op jit(solution)/shard_map/broadcast_in_dim | solution.py:34
  20.5 10.1 %scatter_fusion = f32[160,128,256]{2,1,0:T(8,128)} fusion(f32[160,128,256]{2,1,0:T(8,128)} %broadcast_in_dim.36, s32[32]{0:T(128)S(1)} %fusion.9, f32[32,128,256]{2,1,0:T(8,128)} %copy.14), kind=kCustom, calls=%fused_computation | custom fusion | flops 1048576 | bytes 12583040 | tf_op jit(solution)/shard_map/scatter-add | solution.py:34
  30.6 7.9 %convert_element_type.6 = bf16[160,128,256]{2,1,0:T(8,128)(2,1)S(1)} convert(f32[160,128,256]{2,1,0:T(8,128)} %scatter_fusion) | non-fusion elementwise | flops 5242880 | bytes 31457280 | tf_op jit(solution)/shard_map/convert_element_type | solution.py:35
  38.5 3.8 copy-done.2
  42.4 66.8 %copy.15 = bf16[2,10240,256]{2,0,1:T(2,128)(2,1)} copy(bf16[2,10240,256]{2,1,0:T(8,128)(2,1)S(1)} %bitcast.34) | data formatting | bytes 20971520 | tf_op jit(solution)/shard_map/reshape | solution.py:35
  109.2 6.8 %all-to-all-start = ((bf16[2,10240,256]{2,0,1:T(2,128)(2,1)}), bf16[2,10240,256]{2,0,1:T(2,128)(2,1)}, u32[]{:S(2)}, u32[]{:S(2)}) async-start(bf16[2,10240,256]{2,0,1:T(2,128)(2,1)} %copy.15), calls=%async_computation | async-start | bytes 20971520 | tf_op jit(solution)/shard_map/all_to_all | solution.py:45
  116.0 0.7 slice.72
  116.7 2.0 collective-permute-start
  118.8 0.6 fusion.13
  123.2 0.8 dynamic_slice.12
  124.0 1.3 fusion.12
  125.3 0.7 fusion.11
  126.0 0.1 pad_maximum_fusion
  126.1 1.4 subtract_subtract_fusion
  127.5 0.0 collective-permute-done
  127.5 194.5 %all_gather.3 = bf16[2,16,4096]{2,1,0:T(8,128)(2,1)S(1)} all-gather(bf16[2,16,256]{2,1,0:T(8,128)(2,1)S(1)} %maximum_select_fusion), channel_id=1, replica_groups=mesh['aux'=16,'pair'=2] {'aux'}, dimensions={2}, use_global_device_ids=true | all-gather | bytes 278528 | tf_op jit(solution)/shard_map/all_gather | solution.py:48
  322.0 0.0 all-to-all-done
  322.0 13.8 %copy.16 = bf16[2,640,16,256]{3,2,1,0:T(8,128)(2,1)} copy(bf16[2,640,16,256]{3,0,1,2:T(2,128)(2,1)} %bitcast.6) | data formatting | bytes 20971520 | tf_op jit(solution)/shard_map/all_to_all | solution.py:45
  335.8 16.6 %all_to_all.16 = bf16[2,640,4096]{2,1,0:T(8,128)(2,1)} reshape(bf16[2,640,16,256]{3,2,1,0:T(8,128)(2,1)} %copy.16) | data formatting | bytes 20971520 | tf_op jit(solution)/shard_map/all_to_all | solution.py:45
  352.3 6.8 %fusion.2 = bf16[2,16,640]{2,1,0:T(8,128)(2,1)S(1)} fusion(bf16[2,16,4096]{2,1,0:T(8,128)(2,1)S(1)} %all_gather.3, bf16[2,640,4096]{2,1,0:T(8,128)(2,1)} %all_to_all.16, f32[16,640]{1,0:T(8,128)S(1)} %subtract_subtract_fusion), kind=kOutput, calls=%fused_computation.5 | convolution fusion | flops 167813120 | bytes 10829824 | tf_op jit(solution)/shard_map/owk,osk->ows/dot_general | solution.py:46
  359.1 0.6 slice.73
  359.7 0.1 fusion.6
  359.9 72.5 %psum.7 = f32[8,8]{1,0:T(8,128)S(1)} all-reduce(f32[8,8]{1,0:T(8,128)S(1)} %fusion.7), channel_id=1, replica_groups=mesh['aux'=16,'pair'=2] {'aux','pair'}, use_global_device_ids=true, to_apply=%region_1.2 | all-reduce | flops 64 | bytes 512 | tf_op jit(solution)/shard_map/psum | solution.py:66
  432.4 0.6 broadcast_multiply_fusion
  (9 shorter events, 0.0 us)
Async XLA Ops:
  0.6 1.9 copy-start
  38.5 3.8 copy-start.2
  109.2 9.6 %copy-start.3 = (s32[1,2]{1,0:T(1,128)S(1)}, s32[1,2]{1,0:T(1,128)}, u32[]{:S(2)}) copy-start(s32[1,2]{1,0:T(1,128)} %param.11) | copy-start | bytes 28
  109.2 212.8 %all-to-all-start = ((bf16[2,10240,256]{2,0,1:T(2,128)(2,1)}), bf16[2,10240,256]{2,0,1:T(2,128)(2,1)}, u32[]{:S(2)}, u32[]{:S(2)}) async-start(bf16[2,10240,256]{2,0,1:T(2,128)(2,1)} %copy.15), calls=%async_computation | async-start | bytes 20971520 | tf_op jit(solution)/shard_map/all_to_all | solution.py:45
  116.7 10.8 %collective-permute-start = (bf16[2,8,256]{2,1,0:T(8,128)(2,1)S(1)}, bf16[2,8,256]{2,1,0:T(8,128)(2,1)S(1)}, u32[]{:S(2)}, u32[]{:S(2)}) collective-permute-start(bf16[2,8,256]{2,1,0:T(8,128)(2,1)S(1)} %slice.72), channel_id=1, source_target_pairs={{0,1},{1,0},{2,3},{3,2},{4,5},{5,4},{6,7},{7,6},{8,9},{9,8},{10,11... | collective-permute-start | bytes 24584 | tf_op jit(solution)/shard_map/ppermute | solution.py:15
  335.8 97.2 %copy-start.1 = (bf16[1,1,32,128,128]{4,3,2,1,0:T(8,128)(2,1)S(1)}, bf16[1,1,32,128,128]{4,3,2,1,0:T(8,128)(2,1)}, u32[]{:S(2)}) copy-start(bf16[1,1,32,128,128]{4,3,2,1,0:T(8,128)(2,1)} %param.6) | copy-start | bytes 3145732
where the time goes:
time: 434 us; the launch traced here: 433 us
  blocking collectives  267 us (62%)
  local copies, waits for them, and re-layouts  123 us (28%)
  other arithmetic  20.1 us (5%)
  matrix products  9.59 us (2%)
  starting transfers between devices  8.85 us (2%)
  between operations  4.64 us (1%)
    all_gather x1, blocking collectives, body(): lax.all_gather(window_rows, 'aux', axis=2, tiled=True)  195 us
    psum x1, blocking collectives, body(): density = lax.psum(partial_density, ('aux', 'pair')) / math.sqrt(V)  72.5 us
    reshape x1, local copies, waits for them, and re-layouts, body(): local_rows = summed.astype(jnp.bfloat16).reshape(2, half_width, shard_aux)  66.8 us
    all_to_all x2, local copies, waits for them, and re-layouts, body(): lax.all_to_all(local_rows, 'aux', split_axis=1, concat_axis=2, tiled=True)  30.3 us
    scatter-add x1, other arithmetic, body(): jax.ops.segment_sum(terms, slot_index, num_segments=2 * vblock_count)  10.1 us
    broadcast_in_dim x1, local copies, waits for them, and re-layouts, body(): jax.ops.segment_sum(terms, slot_index, num_segments=2 * vblock_count)  9.61 us
  transfers between devices with their start and end apart: 2, of which 0 were waited for; matrix products, arithmetic and copies ran while one was open for 1% of the time, Pallas kernels for 0%

commit v1 on v0

v1 whole, which is shorter than its diff:
```python
import functools
import math

import jax
import jax.numpy as jnp
from jax import lax
from jax.experimental import pallas as pl
from jax.experimental.pallas import tpu as pltpu
from jax.sharding import PartitionSpec as P

V = 20480
HALF = 8
MESH = pl.DeviceIdType.MESH
F32 = jnp.float32
BF16 = jnp.bfloat16


def table_kernel(nvb, list_ref, occ_ref, pair_ref, tab_ref, eps_ref, inv_ref):
    count = list_ref.shape[0]
    slots = 2 * nvb

    def clear(i, _):
        tab_ref[i] = count
        inv_ref[2 * i] = count
        inv_ref[2 * i + 1] = count
        return 0

    lax.fori_loop(0, slots, clear, 0, unroll=8)

    def place(e, _):
        o = list_ref[e, 0]
        v = list_ref[e, 1]
        k = list_ref[e, 2]

        @pl.when(o >= 0)
        def _():
            inv_ref[2 * (o * nvb + v) + k] = e
            tab_ref[(1 - o) * nvb + v] = e

        return 0

    lax.fori_loop(0, count, place, 0)

    def partners(e, _):
        o = list_ref[e, 0]
        v = list_ref[e, 1]
        live = o >= 0
        at = jnp.where(live, 2 * (o * nvb + v), 0)
        tab_ref[slots + e] = jnp.where(live, inv_ref[at], count)
        tab_ref[slots + count + e] = jnp.where(live, inv_ref[at + 1], count)
        return 0

    lax.fori_loop(0, count, partners, 0)
    for o in range(2):
        for k in range(2):
            tab_ref[slots + 2 * count + 2 * o + k] = inv_ref[2 * o * nvb + k]
    q = lax.axis_index("pair") // 2
    eps_ref[0] = occ_ref[pair_ref[q, 0]]
    eps_ref[1] = occ_ref[pair_ref[q, 1]]


def main_kernel(
    n_aux, n_pair, nvb, slab, nb,
    tab_ref, eps_ref, blocks_ref, metric_ref, ven_ref,
    amp_ref, den_ref,
    held, three, part, wsend, wrecv, csend, crecv, dsend, drecv, psum_buf, asum_buf,
    load_sem, w_sems, cs_sems, cr_sems, ds_sems, dr_sems, ps_sems, pr_sems, as_sems, ar_sems,
):
    count = blocks_ref.shape[0]
    lanes = blocks_ref.shape[1]
    slots = 2 * nvb
    n_t = n_aux // 2
    me = lax.axis_index("aux")
    p = lax.axis_index("pair")
    core = me % 2
    my_t = me // 2
    half = p % 2
    mate = p + 1 - 2 * half
    other = me + 1 - 2 * core

    load = pltpu.make_async_copy(blocks_ref, held.at[pl.ds(0, count)], load_sem)
    load.start()

    psum_buf[...] = jnp.zeros_like(psum_buf)
    barrier = pltpu.get_barrier_semaphore()

    def greet_aux(s, _):
        pl.semaphore_signal(barrier, inc=1, device_id=((me + s) % n_aux, p), device_id_type=MESH)
        return 0

    def greet_pair(s, _):
        pl.semaphore_signal(barrier, inc=1, device_id=(me, (p + s) % n_pair), device_id_type=MESH)
        return 0

    lax.fori_loop(1, n_pair, greet_pair, 0)
    lax.fori_loop(1, n_aux, greet_aux, 0)

    held[count] = jnp.zeros(held.shape[1:], BF16)
    part[count] = jnp.zeros(part.shape[1:], F32)
    load.wait()
    own = [
        held[tab_ref[slots + 2 * count + i], :16, :].astype(F32)[:HALF] for i in range(4)
    ]
    wsend[...] = jnp.concatenate(own, axis=0).astype(BF16)
    pl.semaphore_wait(barrier, n_aux + n_pair - 2)
    wcopy = pltpu.make_async_remote_copy(
        src_ref=wsend, dst_ref=wrecv, send_sem=w_sems.at[0], recv_sem=w_sems.at[1],
        device_id=(me, mate), device_id_type=MESH,
    )
    wcopy.start()

    metric = metric_ref[...]

    def transform(e, _):
        rows = jnp.concatenate(
            [held[tab_ref[slots + e]], held[tab_ref[slots + count + e]]], axis=1
        )
        three[e] = jnp.dot(rows, metric, preferred_element_type=F32).astype(BF16)
        return 0

    lax.fori_loop(0, count, transform, 0, unroll=4)

    wcopy.wait()
    theirs = wrecv[...].astype(F32)
    rows = []
    for o in range(2):
        mine = jnp.concatenate([own[2 * o], own[2 * o + 1]], axis=1)
        got = jnp.concatenate(
            [theirs[16 * o : 16 * o + HALF], theirs[16 * o + HALF : 16 * o + 16]], axis=1
        )
        rows.append(jnp.where(half == 0, mine, got))
        rows.append(jnp.where(half == 0, got, mine))
    window = jnp.dot(
        jnp.concatenate(rows, axis=0).astype(BF16), metric, preferred_element_type=F32
    ).astype(BF16)

    def contract(e, _):
        part[e] = lax.dot_general(
            window, three[e], (((1,), (1,)), ((), ())), preferred_element_type=F32
        )
        return 0

    lax.fori_loop(0, count, contract, 0, unroll=4)

    def first_block(d):
        return (d * slab) // lanes

    def piece(d, c, j):
        return part[tab_ref[c * nvb + first_block(d) + j], 16 * c : 16 * (c + 1), :]

    def c_copy(t):
        return pltpu.make_async_remote_copy(
            src_ref=csend.at[t], dst_ref=crecv.at[t],
            send_sem=cs_sems.at[t], recv_sem=cr_sems.at[t],
            device_id=(other, p), device_id_type=MESH,
        )

    def d_copy(t, slot):
        return pltpu.make_async_remote_copy(
            src_ref=dsend.at[t], dst_ref=drecv.at[slot],
            send_sem=ds_sems.at[t], recv_sem=dr_sems.at[slot],
            device_id=(2 * t + core, p), device_id_type=MESH,
        )

    def to_core(s, _):
        t = (my_t + s) % n_t
        d = 2 * t + 1 - core
        for c in range(2):
            for j in range(nb):
                csend[t, 16 * c : 16 * (c + 1), lanes * j : lanes * (j + 1)] = piece(d, c, j)
        c_copy(t).start()
        return 0

    lax.fori_loop(1, n_t + 1, to_core, 0)

    def to_chip(s, _):
        t = (my_t + s) % n_t
        d = 2 * t + core
        c_copy(t).wait_recv()
        for c in range(2):
            for j in range(nb):
                here = (slice(16 * c, 16 * (c + 1)), slice(lanes * j, lanes * (j + 1)))
                dsend[(t,) + here] = (piece(d, c, j) + crecv[(t,) + here]).astype(BF16)
        d_copy(t, my_t).start()
        return 0

    lax.fori_loop(1, n_t, to_chip, 0)
    c_copy(my_t).wait_recv()

    first = first_block(me)
    offset = me * slab - first * lanes
    sub = lax.broadcasted_iota(jnp.int32, (16, lanes), 0)
    lane = lax.broadcasted_iota(jnp.int32, (16, lanes), 1)
    tops = jnp.where(sub < HALF, ven_ref[0:1, :], ven_ref[nvb : nvb + 1, :])
    column = jnp.sum(jnp.where(lane == sub % HALF, tops, 0.0), axis=1, keepdims=True)

    totals = []
    for c in range(2):
        for j in range(nb):
            here = (slice(16 * c, 16 * (c + 1)), slice(lanes * j, lanes * (j + 1)))
            totals.append(piece(me, c, j) + crecv[(my_t,) + here])

    def arrive(s, totals):
        t = (my_t + n_t - s) % n_t
        pltpu.make_async_remote_copy(
            src_ref=dsend.at[t], dst_ref=drecv.at[t],
            send_sem=ds_sems.at[t], recv_sem=dr_sems.at[t],
            device_id=(2 * t + core, p), device_id_type=MESH,
        ).wait_recv()
        out = []
        for c in range(2):
            for j in range(nb):
                here = (slice(16 * c, 16 * (c + 1)), slice(lanes * j, lanes * (j + 1)))
                out.append(totals[c * nb + j] + drecv[(t,) + here].astype(F32))
        return tuple(out)

    totals = lax.fori_loop(1, n_t, arrive, tuple(totals))

    grams = [[jnp.zeros((HALF, HALF), F32) for _ in range(2)] for _ in range(2)]
    for j in range(nb):
        energy = ven_ref[pl.ds(half * nvb + first + j, 1), :]
        denominator = column + energy - eps_ref[0] - eps_ref[1]
        heads, tails = [], []
        for c in range(2):
            scaled = (totals[c * nb + j] / denominator).astype(BF16)
            if c == 0:
                amp_ref[:, lanes * j : lanes * (j + 1)] = scaled
            wide = scaled.astype(F32)
            if slab % lanes:
                at = lane + (j * lanes - offset)
                wide = jnp.where(jnp.logical_and(at >= 0, at < slab), wide, 0.0)
            heads.append(wide[:HALF].astype(BF16))
            tails.append(wide[HALF:].astype(BF16))
        for a in range(2):
            for b in range(2):
                grams[a][b] += lax.dot_general(
                    heads[a], tails[b], (((1,), (1,)), ((), ())), preferred_element_type=F32
                )
    psum_buf[p, :, :HALF] = (
        2.0 * (grams[0][0] + grams[1][1]) - grams[1][0] - grams[0][1]
    )

    def p_copy(q, slot):
        return pltpu.make_async_remote_copy(
            src_ref=psum_buf.at[p], dst_ref=psum_buf.at[slot],
            send_sem=ps_sems.at[q], recv_sem=pr_sems.at[slot],
            device_id=(me, q), device_id_type=MESH,
        )

    def p_send(s, _):
        p_copy((p + s) % n_pair, p).start()
        return 0

    lax.fori_loop(1, n_pair, p_send, 0)

    def p_wait(s, _):
        q = (p + s) % n_pair
        p_copy(q, q).wait()
        return 0

    lax.fori_loop(1, n_pair, p_wait, 0)
    total = psum_buf[0]
    for q in range(1, n_pair):
        total = total + psum_buf[q]
    asum_buf[me] = total

    def a_copy(d, slot):
        return pltpu.make_async_remote_copy(
            src_ref=asum_buf.at[me], dst_ref=asum_buf.at[slot],
            send_sem=as_sems.at[d], recv_sem=ar_sems.at[slot],
            device_id=(d, p), device_id_type=MESH,
        )

    def a_send(s, _):
        a_copy((me + s) % n_aux, me).start()
        return 0

    lax.fori_loop(1, n_aux, a_send, 0)

    def sent(s, _):
        t = (my_t + s) % n_t
        d_copy(t, my_t).wait_send()
        c_copy(t).wait_send()
        return 0

    lax.fori_loop(1, n_t, sent, 0)
    c_copy(my_t).wait_send()

    def a_wait(s, _):
        d = (me + s) % n_aux
        a_copy(d, d).wait()
        return 0

    lax.fori_loop(1, n_aux, a_wait, 0)
    total = asum_buf[0]
    for d in range(1, n_aux):
        total = total + asum_buf[d]
    den_ref[...] = (total / math.sqrt(V))[:, :HALF]


def body(blocks, block_list, metric, virt_energy, occ_energy, pair_list):
    n_aux = lax.axis_size("aux")
    n_pair = lax.axis_size("pair")
    raw = blocks[0, 0]
    entries = block_list[0, 0]
    count, lanes = raw.shape[0], raw.shape[1]
    width = virt_energy.shape[0] // 2
    nvb = width // lanes
    slab = width // n_aux
    nb = max(-(-((d + 1) * slab) // lanes) - d * slab // lanes for d in range(n_aux))
    shard = metric.shape[1]
    n_t = n_aux // 2
    vmem = pl.BlockSpec(memory_space=pltpu.VMEM)
    smem = pl.BlockSpec(memory_space=pltpu.SMEM)
    table, eps = pl.pallas_call(
        functools.partial(table_kernel, nvb),
        out_shape=(
            jax.ShapeDtypeStruct((2 * nvb + 2 * count + 4,), jnp.int32),
            jax.ShapeDtypeStruct((2,), F32),
        ),
        in_specs=[smem] * 3,
        out_specs=(smem, smem),
        scratch_shapes=[pltpu.SMEM((4 * nvb,), jnp.int32)],
        name="tables",
    )(entries, occ_energy, pair_list)
    dma = pltpu.SemaphoreType.DMA
    amp, density = pl.pallas_call(
        functools.partial(main_kernel, n_aux, n_pair, nvb, slab, nb),
        out_shape=(
            jax.ShapeDtypeStruct((2 * HALF, nb * lanes), BF16),
            jax.ShapeDtypeStruct((HALF, HALF), F32),
        ),
        in_specs=[smem, smem, pl.BlockSpec(memory_space=pl.ANY), vmem, vmem],
        out_specs=(vmem, vmem),
        scratch_shapes=[
            pltpu.VMEM((count + 1, lanes, raw.shape[2]), BF16),
            pltpu.VMEM((count, lanes, shard), BF16),
            pltpu.VMEM((count + 1, 32, lanes), F32),
            pltpu.VMEM((32, lanes), BF16),
            pltpu.VMEM((32, lanes), BF16),
            pltpu.VMEM((n_t, 32, nb * lanes), F32),
            pltpu.VMEM((n_t, 32, nb * lanes), F32),
            pltpu.VMEM((n_t, 32, nb * lanes), BF16),
            pltpu.VMEM((n_t, 32, nb * lanes), BF16),
            pltpu.VMEM((n_pair, HALF, lanes), F32),
            pltpu.VMEM((n_aux, HALF, lanes), F32),
            dma,
            dma((2,)),
            dma((n_t,)),
            dma((n_t,)),
            dma((n_t,)),
            dma((n_t,)),
            dma((n_pair,)),
            dma((n_pair,)),
            dma((n_aux,)),
            dma((n_aux,)),
        ],
        compiler_params=pltpu.CompilerParams(
            collective_id=0, has_side_effects=True, vmem_limit_bytes=40 * 2**20
        ),
        name="amplitudes",
    )(table, eps, raw, metric, virt_energy.reshape(-1, lanes))
    if slab % lanes:
        me = lax.axis_index("aux")
        amp = lax.dynamic_slice_in_dim(amp, me * slab - me * slab // lanes * lanes, slab, 1)
    return (amp[None], density)


def solution(mesh):
    in_specs = (
        P("aux", "pair", None, None, None),
        P("aux", "pair", None, None),
        P("aux", None),
        P(),
        P(),
        P(),
    )
    out_specs = (P("pair", None, "aux"), P())
    return jax.shard_map(body, mesh=mesh, in_specs=in_specs, out_specs=out_specs, check_vma=False)
```

time: 434 us -> 39.8 us (0.09)
  blocking collectives: 267 us -> 0 us
  local copies, waits for them, and re-layouts: 123 us -> 6.25 us
  Pallas kernels: 0 us -> 32.5 us
  other arithmetic: 20.1 us -> 0 us
  matrix products: 9.59 us -> 0 us
  starting transfers between devices: 8.85 us -> 0 us
    all_gather x1 -> x0, blocking collectives: 195 us -> none  [body(): lax.all_gather(window_rows, 'aux', axis=2, tiled=True)]
    psum x1 -> x0, blocking collectives: 72.5 us -> none  [body(): density = lax.psum(partial_density, ('aux', 'pair')) / math.sqrt(V)]
    reshape x1 -> x0, local copies, waits for them, and re-layouts: 66.8 us -> none  [body(): local_rows = summed.astype(jnp.bfloat16).reshape(2, half_width, shard_aux)]
    pallas_call x0 -> x2, Pallas kernels: none -> 32.5 us  [the longest x1 29.3 us: body(): pl.pallas_call(functools.partial(main_kernel, n_aux, n_pair, nvb, slab, n...]
    all_to_all x2 -> x0, local copies, waits for them, and re-layouts: 30.3 us -> none  [body(): lax.all_to_all(local_rows, 'aux', split_axis=1, concat_axis=2, tiled=True)]
    scatter-add x1 -> x0, other arithmetic: 10.1 us -> none  [body(): jax.ops.segment_sum(terms, slot_index, num_segments=2 * vblock_count)]
    broadcast_in_dim x1 -> x0, local copies, waits for them, and re-layouts: 9.61 us -> none  [body(): jax.ops.segment_sum(terms, slot_index, num_segments=2 * vblock_count)]
    dot_general x3 -> x0, matrix products: 9.59 us -> none  [the longest x1 6.78 us: body(): jnp.einsum('owk,osk->ows', lax.all_gather(window_rows, 'aux', axis=2, til...]
  transfers between devices with their start and end apart: 2 -> 0, of which waited for: 0 -> 0; matrix products, arithmetic and copies ran while one was open for 1% -> 0% of each run, Pallas kernels for 0% -> 0%
where the time goes in v1:
time: 39.8 us; the launch traced here: 39.4 us
  Pallas kernels  32.5 us (82%)
  local copies, waits for them, and re-layouts  6.25 us (16%)
  between operations  0.67 us (2%)
    pallas_call x1, Pallas kernels, body(): pl.pallas_call(functools.partial(main_kernel, n_aux, n_pair, nvb, slab, n...  29.3 us
    unnamed x14, local copies, waits for them, and re-layouts  5.56 us
    pallas_call x1, Pallas kernels, body(): pl.pallas_call(functools.partial(table_kernel, nvb), out_shape=(jax.Shape...  3.19 us

profile of v1, /device:TPU:0, one launch (start us, length us, event | category | flops | bytes accessed | tf_op | source)
XLA Modules:
  0.0 39.4 jit_solution(1695060845126680055)
XLA Ops:
  0.6 0.0 copy-start.5
  0.6 0.7 %copy-done.5 = s32[1,1,32,3]{2,1,3,0:T(1,128)S(1)} copy-done((s32[1,1,32,3]{2,1,3,0:T(1,128)S(1)}, s32[1,1,32,3]{2,1,3,0:T(1,128)}, u32[]{:S(2)}) %copy-start.5) | copy-done | bytes 408
  1.3 0.7 %copy.9 = s32[1,1,32,3]{3,2,1,0:T(8,128)} copy(s32[1,1,32,3]{2,1,3,0:T(1,128)S(1)} %copy-done.5) | data formatting | bytes 768 | tf_op jit(solution)/shard_map/squeeze | solution.py:305
  2.0 3.2 %tables.1 = (s32[228]{0:T(256)}, f32[2]{0:T(128)}) custom-call(s32[32,3]{1,0:T(8,128)} %bitcast.7, f32[8000]{0:T(1024)} %occ_ref.1, s32[1,2]{1,0:T(1,128)} %pair_ref.1), custom_call_target="tpu_custom_call" | custom-call | tf_op jit(solution)/shard_map/tables/pallas_call | solution.py:315
  5.2 0.0 copy-start.3
  5.2 0.0 copy-start.4
  5.2 0.7 %copy-done.3 = s32[228]{0:T(256)S(1)} copy-done((s32[228]{0:T(256)S(1)}, s32[228]{0:T(256)}, u32[]{:S(2)}) %copy-start.3) | copy-done | bytes 936
  5.9 0.0 copy-done.4
  5.9 0.0 copy-start
  5.9 1.2 %copy-done = bf16[1,1,32,128,128]{4,3,2,1,0:T(8,128)(2,1)S(1)} copy-done((bf16[1,1,32,128,128]{4,3,2,1,0:T(8,128)(2,1)S(1)}, bf16[1,1,32,128,128]{4,3,2,1,0:T(8,128)(2,1)}, u32[]{:S(2)}) %copy-start) | copy-done | bytes 1048600
  7.1 0.0 copy-start.1
  7.1 0.9 %copy-done.1 = bf16[256,256]{1,0:T(8,128)(2,1)S(1)} copy-done((bf16[256,256]{1,0:T(8,128)(2,1)S(1)}, bf16[256,256]{1,0:T(8,128)(2,1)}, u32[]{:S(2)}) %copy-start.1) | copy-done | bytes 131096
  8.0 0.0 copy-start.2
  8.0 0.9 %copy-done.2 = f32[20480]{0:T(1024)S(1)} copy-done((f32[20480]{0:T(1024)S(1)}, f32[20480]{0:T(1024)}, u32[]{:S(2)}) %copy-start.2) | copy-done | bytes 81944
  8.9 29.3 %amplitudes.1 = (bf16[16,640]{1,0:T(8,128)(2,1)S(1)}, f32[8,8]{1,0:T(8,128)S(1)}) custom-call(s32[228]{0:T(256)S(1)} %copy-done.3, f32[2]{0:T(128)S(1)} %copy-done.4, bf16[32,128,128]{2,1,0:T(8,128)(2,1)S(1)} %bitcast.4, bf16[256,256]{1,0:T(8,128)(2,1)S(1)} %copy-done.1, f32[160,128]{1,0:T(8,128)S(1)} %bitcast.5), custom_call_target="tpu_custom_call" | custom-call | tf_op jit(solution)/shard_map/amplitudes/pallas_call | solution.py:327
  38.2 0.6 %copy.12 = bf16[1,16,640]{2,1,0:T(8,128)(2,1)} copy(bf16[1,16,640]{2,1,0:T(8,128)(2,1)S(1)} %bitcast.6) | data formatting | bytes 40960
  38.8 0.6 %copy.13 = f32[8,8]{1,0:T(8,128)} copy(f32[8,8]{1,0:T(8,128)S(1)} %get-tuple-element.13) | data formatting | bytes 512
Async XLA Ops:
  0.6 0.7 %copy-start.5 = (s32[1,1,32,3]{2,1,3,0:T(1,128)S(1)}, s32[1,1,32,3]{2,1,3,0:T(1,128)}, u32[]{:S(2)}) copy-start(s32[1,1,32,3]{2,1,3,0:T(1,128)} %param.7) | copy-start | bytes 1156
  5.2 0.7 %copy-start.3 = (s32[228]{0:T(256)S(1)}, s32[228]{0:T(256)}, u32[]{:S(2)}) copy-start(s32[228]{0:T(256)} %get-tuple-element.6.tab_ref) | copy-start | bytes 2740
  5.2 0.7 %copy-start.4 = (f32[2]{0:T(128)S(1)}, f32[2]{0:T(128)}, u32[]{:S(2)}) copy-start(f32[2]{0:T(128)} %get-tuple-element.7.eps_ref) | copy-start | bytes 28
  5.9 1.2 %copy-start = (bf16[1,1,32,128,128]{4,3,2,1,0:T(8,128)(2,1)S(1)}, bf16[1,1,32,128,128]{4,3,2,1,0:T(8,128)(2,1)}, u32[]{:S(2)}) copy-start(bf16[1,1,32,128,128]{4,3,2,1,0:T(8,128)(2,1)} %param.6) | copy-start | bytes 3145732
  7.1 0.9 %copy-start.1 = (bf16[256,256]{1,0:T(8,128)(2,1)S(1)}, bf16[256,256]{1,0:T(8,128)(2,1)}, u32[]{:S(2)}) copy-start(bf16[256,256]{1,0:T(8,128)(2,1)} %metric_ref.1) | copy-start | bytes 393220
  8.0 0.9 %copy-start.2 = (f32[20480]{0:T(1024)S(1)}, f32[20480]{0:T(1024)}, u32[]{:S(2)}) copy-start(f32[20480]{0:T(1024)} %param.9) | copy-start | bytes 245764

commit v2 on v1

--- a/solution.py
+++ b/solution.py
@@ -15,60 +15,41 @@
 BF16 = jnp.bfloat16
 
 
-def table_kernel(nvb, list_ref, occ_ref, pair_ref, tab_ref, eps_ref, inv_ref):
-    count = list_ref.shape[0]
-    slots = 2 * nvb
-
-    def clear(i, _):
-        tab_ref[i] = count
-        inv_ref[2 * i] = count
-        inv_ref[2 * i + 1] = count
-        return 0
-
-    lax.fori_loop(0, slots, clear, 0, unroll=8)
-
-    def place(e, _):
-        o = list_ref[e, 0]
-        v = list_ref[e, 1]
-        k = list_ref[e, 2]
-
-        @pl.when(o >= 0)
-        def _():
-            inv_ref[2 * (o * nvb + v) + k] = e
-            tab_ref[(1 - o) * nvb + v] = e
-
-        return 0
-
-    lax.fori_loop(0, count, place, 0)
-
-    def partners(e, _):
-        o = list_ref[e, 0]
-        v = list_ref[e, 1]
-        live = o >= 0
-        at = jnp.where(live, 2 * (o * nvb + v), 0)
-        tab_ref[slots + e] = jnp.where(live, inv_ref[at], count)
-        tab_ref[slots + count + e] = jnp.where(live, inv_ref[at + 1], count)
-        return 0
-
-    lax.fori_loop(0, count, partners, 0)
-    for o in range(2):
-        for k in range(2):
-            tab_ref[slots + 2 * count + 2 * o + k] = inv_ref[2 * o * nvb + k]
-    q = lax.axis_index("pair") // 2
-    eps_ref[0] = occ_ref[pair_ref[q, 0]]
-    eps_ref[1] = occ_ref[pair_ref[q, 1]]
+def index_table(nvb, count, list_ref):
+    row = lax.broadcasted_iota(jnp.int32, (8, 128), 0)
+    lane = lax.broadcasted_iota(jnp.int32, (8, 128), 1)
+
+    def slot_of(e):
+        o = list_ref[0, 0, e]
+        return jnp.where(o >= 0, o * nvb + list_ref[1, 0, e], -1)
+
+    def spread(e, slots):
+        return jnp.where(lane == e, slot_of(e), slots)
+
+    slots = lax.fori_loop(0, count, spread, jnp.full((8, 128), -2, jnp.int32), unroll=8)
+    slots = jnp.where(slots < 0, -2, slots)
+    by_block = jnp.where(lane < nvb, jnp.where(row == 0, nvb + lane, lane), -2)
+    by_window = jnp.where(lane < 4, jnp.where(lane < 2, 0, nvb), -2)
+    key = jnp.where(row < 2, by_block, jnp.where(row < 4, slots, by_window))
+    aux = jnp.where(row < 2, -1, jnp.where(row < 4, row - 2, jnp.bitwise_and(lane, 1)))
+
+    def enter(e, table):
+        hit = (key == slot_of(e)) & ((aux < 0) | (aux == list_ref[2, 0, e]))
+        return jnp.where(hit, e, table)
+
+    return lax.fori_loop(0, count, enter, jnp.full((8, 128), count, jnp.int32), unroll=8)
 
 
 def main_kernel(
     n_aux, n_pair, nvb, slab, nb,
-    tab_ref, eps_ref, blocks_ref, metric_ref, ven_ref,
+    list_hbm, occ_hbm, pair_hbm, blocks_ref, metric_hbm, ven_hbm,
     amp_ref, den_ref,
+    list_ref, occ_ref, pair_ref, metric_ref, ven_ref, tab_vmem, tab_ref,
     held, three, part, wsend, wrecv, csend, crecv, dsend, drecv, psum_buf, asum_buf,
-    load_sem, w_sems, cs_sems, cr_sems, ds_sems, dr_sems, ps_sems, pr_sems, as_sems, ar_sems,
+    load_sems, w_sems, cs_sems, cr_sems, ds_sems, dr_sems, ps_sems, pr_sems, as_sems, ar_sems,
 ):
     count = blocks_ref.shape[0]
     lanes = blocks_ref.shape[1]
-    slots = 2 * nvb
     n_t = n_aux // 2
     me = lax.axis_index("aux")
     p = lax.axis_index("pair")
@@ -78,8 +59,19 @@
     mate = p + 1 - 2 * half
     other = me + 1 - 2 * core
 
-    load = pltpu.make_async_copy(blocks_ref, held.at[pl.ds(0, count)], load_sem)
-    load.start()
+    loads = [
+        pltpu.make_async_copy(src, dst, load_sems.at[i])
+        for i, (src, dst) in enumerate([
+            (list_hbm, list_ref),
+            (blocks_ref, held.at[pl.ds(0, count)]),
+            (metric_hbm, metric_ref),
+            (pair_hbm, pair_ref),
+            (occ_hbm, occ_ref),
+            (ven_hbm, ven_ref),
+        ])
+    ]
+    for load in loads:
+        load.start()
 
     psum_buf[...] = jnp.zeros_like(psum_buf)
     barrier = pltpu.get_barrier_semaphore()
@@ -97,10 +89,13 @@
 
     held[count] = jnp.zeros(held.shape[1:], BF16)
     part[count] = jnp.zeros(part.shape[1:], F32)
-    load.wait()
-    own = [
-        held[tab_ref[slots + 2 * count + i], :16, :].astype(F32)[:HALF] for i in range(4)
-    ]
+    loads[0].wait()
+    tab_vmem[...] = index_table(nvb, count, list_ref)
+    fill = pltpu.make_async_copy(tab_vmem, tab_ref, load_sems.at[len(loads)])
+    fill.start()
+    loads[1].wait()
+    fill.wait()
+    own = [held[tab_ref[4, i], :16, :].astype(F32)[:HALF] for i in range(4)]
     wsend[...] = jnp.concatenate(own, axis=0).astype(BF16)
     pl.semaphore_wait(barrier, n_aux + n_pair - 2)
     wcopy = pltpu.make_async_remote_copy(
@@ -109,11 +104,12 @@
     )
     wcopy.start()
 
+    loads[2].wait()
     metric = metric_ref[...]
 
     def transform(e, _):
         rows = jnp.concatenate(
-            [held[tab_ref[slots + e]], held[tab_ref[slots + count + e]]], axis=1
+            [held[tab_ref[2, e]], held[tab_ref[3, e]]], axis=1
         )
         three[e] = jnp.dot(rows, metric, preferred_element_type=F32).astype(BF16)
         return 0
@@ -146,7 +142,7 @@
         return (d * slab) // lanes
 
     def piece(d, c, j):
-        return part[tab_ref[c * nvb + first_block(d) + j], 16 * c : 16 * (c + 1), :]
+        return part[tab_ref[c, first_block(d) + j], 16 * c : 16 * (c + 1), :]
 
     def c_copy(t):
         return pltpu.make_async_remote_copy(
@@ -187,6 +183,10 @@
     lax.fori_loop(1, n_t, to_chip, 0)
     c_copy(my_t).wait_recv()
 
+    for load in loads[3:]:
+        load.wait()
+    first_energy = occ_ref[pair_ref[p // 2, 0]]
+    second_energy = occ_ref[pair_ref[p // 2, 1]]
     first = first_block(me)
     offset = me * slab - first * lanes
     sub = lax.broadcasted_iota(jnp.int32, (16, lanes), 0)
@@ -219,7 +219,7 @@
     grams = [[jnp.zeros((HALF, HALF), F32) for _ in range(2)] for _ in range(2)]
     for j in range(nb):
         energy = ven_ref[pl.ds(half * nvb + first + j, 1), :]
-        denominator = column + energy - eps_ref[0] - eps_ref[1]
+        denominator = column + energy - first_energy - second_energy
         heads, tails = [], []
         for c in range(2):
             scaled = (totals[c * nb + j] / denominator).astype(BF16)
@@ -302,7 +302,7 @@
     n_aux = lax.axis_size("aux")
     n_pair = lax.axis_size("pair")
     raw = blocks[0, 0]
-    entries = block_list[0, 0]
+    entries = jnp.transpose(block_list[0], (2, 0, 1))
     count, lanes = raw.shape[0], raw.shape[1]
     width = virt_energy.shape[0] // 2
     nvb = width // lanes
@@ -311,18 +311,7 @@
     shard = metric.shape[1]
     n_t = n_aux // 2
     vmem = pl.BlockSpec(memory_space=pltpu.VMEM)
-    smem = pl.BlockSpec(memory_space=pltpu.SMEM)
-    table, eps = pl.pallas_call(
-        functools.partial(table_kernel, nvb),
-        out_shape=(
-            jax.ShapeDtypeStruct((2 * nvb + 2 * count + 4,), jnp.int32),
-            jax.ShapeDtypeStruct((2,), F32),
-        ),
-        in_specs=[smem] * 3,
-        out_specs=(smem, smem),
-        scratch_shapes=[pltpu.SMEM((4 * nvb,), jnp.int32)],
-        name="tables",
-    )(entries, occ_energy, pair_list)
+    hbm = pl.BlockSpec(memory_space=pltpu.HBM)
     dma = pltpu.SemaphoreType.DMA
     amp, density = pl.pallas_call(
         functools.partial(main_kernel, n_aux, n_pair, nvb, slab, nb),
@@ -330,9 +319,16 @@
             jax.ShapeDtypeStruct((2 * HALF, nb * lanes), BF16),
             jax.ShapeDtypeStruct((HALF, HALF), F32),
         ),
-        in_specs=[smem, smem, pl.BlockSpec(memory_space=pl.ANY), vmem, vmem],
+        in_specs=[hbm] * 6,
         out_specs=(vmem, vmem),
         scratch_shapes=[
+            pltpu.SMEM((3, 1, count), jnp.int32),
+            pltpu.SMEM(occ_energy.shape, F32),
+            pltpu.SMEM(pair_list.shape, jnp.int32),
+            pltpu.VMEM(metric.shape, BF16),
+            pltpu.VMEM((2 * nvb, lanes), F32),
+            pltpu.VMEM((8, 128), jnp.int32),
+            pltpu.SMEM((8, 128), jnp.int32),
             pltpu.VMEM((count + 1, lanes, raw.shape[2]), BF16),
             pltpu.VMEM((count, lanes, shard), BF16),
             pltpu.VMEM((count + 1, 32, lanes), F32),
@@ -344,7 +340,7 @@
             pltpu.VMEM((n_t, 32, nb * lanes), BF16),
             pltpu.VMEM((n_pair, HALF, lanes), F32),
             pltpu.VMEM((n_aux, HALF, lanes), F32),
-            dma,
+            dma((7,)),
             dma((2,)),
             dma((n_t,)),
             dma((n_t,)),
@@ -356,10 +352,10 @@
             dma((n_aux,)),
         ],
         compiler_params=pltpu.CompilerParams(
-            collective_id=0, has_side_effects=True, vmem_limit_bytes=40 * 2**20
+            collective_id=0, has_side_effects=True, vmem_limit_bytes=60 * 2**20
         ),
         name="amplitudes",
-    )(table, eps, raw, metric, virt_energy.reshape(-1, lanes))
+    )(entries, occ_energy, pair_list, raw, metric, virt_energy.reshape(-1, lanes))
     if slab % lanes:
         me = lax.axis_index("aux")
         amp = lax.dynamic_slice_in_dim(amp, me * slab - me * slab // lanes * lanes, slab, 1)

time: 39.8 us -> 32.1 us (0.81)
  local copies, waits for them, and re-layouts: 6.25 us -> 1.93 us
  Pallas kernels: 32.5 us -> 29.3 us
    unnamed x14 -> x4, local copies, waits for them, and re-layouts: 5.56 us -> 1.93 us
    pallas_call x1 -> x0, Pallas kernels: 3.19 us -> none  [body(): pl.pallas_call(functools.partial(table_kernel, nvb), out_shape=(jax.Shape...]
    squeeze x1 -> x0, local copies, waits for them, and re-layouts: 0.69 us -> none  [body(): entries = block_list[0, 0]]
where the time goes in v2:
time: 32.1 us; the launch traced here: 31.9 us
  Pallas kernels  29.3 us (91%)
  local copies, waits for them, and re-layouts  1.93 us (6%)
  between operations  0.65 us (2%)
    pallas_call x1, Pallas kernels, body(): pl.pallas_call(functools.partial(main_kernel, n_aux, n_pair, nvb, slab, n...  29.3 us
    unnamed x4, local copies, waits for them, and re-layouts  1.93 us

profile of v2, /device:TPU:0, one launch (start us, length us, event | category | flops | bytes accessed | tf_op | source)
XLA Modules:
  0.0 31.9 jit_solution(15482556755727812793)
XLA Ops:
  0.6 29.3 %amplitudes.1 = (bf16[16,640]{1,0:T(8,128)(2,1)}, f32[8,8]{1,0:T(8,128)}) custom-call(s32[3,1,32]{2,1,0:T(1,128)} %bitcast.9, f32[8000]{0:T(1024)} %occ_hbm.1, s32[1,2]{1,0:T(1,128)} %pair_hbm.1, bf16[32,128,128]{2,1,0:T(8,128)(2,1)} %bitcast.6, bf16[256,256]{1,0:T(8,128)(2,1)} %metric_hbm.1, f32[160,128]{1,0:T(8,128)} %bitcast.7), custom_call_target="tpu_custom_call" | custom-call | tf_op jit(solution)/shard_map/amplitudes/pallas_call | solution.py:316
  30.0 0.0 copy-start
  30.0 1.3 %copy.10 = bf16[1,16,640]{2,1,0:T(8,128)(2,1)} copy(bf16[1,16,640]{2,1,0:T(8,128)(2,1)} %bitcast.8) | data formatting | bytes 40960
  31.3 0.0 copy-done
  31.3 0.6 %copy.11 = f32[8,8]{1,0:T(8,128)} copy(f32[8,8]{1,0:T(8,128)S(1)} %copy-done) | data formatting | bytes 512
Async XLA Ops:
  30.0 1.3 %copy-start = (f32[8,8]{1,0:T(8,128)S(1)}, f32[8,8]{1,0:T(8,128)}, u32[]{:S(2)}) copy-start(f32[8,8]{1,0:T(8,128)} %get-tuple-element.9) | copy-start | bytes 772

commit v3 on v2

--- a/solution.py
+++ b/solution.py
@@ -15,6 +15,10 @@
 BF16 = jnp.bfloat16
 
 
+def wrap(i, n):
+    return jnp.where(i >= n, i - n, i)
+
+
 def index_table(nvb, count, list_ref):
     row = lax.broadcasted_iota(jnp.int32, (8, 128), 0)
     lane = lax.broadcasted_iota(jnp.int32, (8, 128), 1)
@@ -45,8 +49,8 @@
     list_hbm, occ_hbm, pair_hbm, blocks_ref, metric_hbm, ven_hbm,
     amp_ref, den_ref,
     list_ref, occ_ref, pair_ref, metric_ref, ven_ref, tab_vmem, tab_ref,
-    held, three, part, wsend, wrecv, csend, crecv, dsend, drecv, psum_buf, asum_buf,
-    load_sems, w_sems, cs_sems, cr_sems, ds_sems, dr_sems, ps_sems, pr_sems, as_sems, ar_sems,
+    held, three, part, wsend, wrecv, csend, crecv, xsend, xrecv, zsend, zrecv, sums,
+    load_sems, w_sems, cs_sems, cr_sems, xs_sems, xr_sems, zs_sems, zr_sems, sum_sems,
 ):
     count = blocks_ref.shape[0]
     lanes = blocks_ref.shape[1]
@@ -55,6 +59,9 @@
     p = lax.axis_index("pair")
     core = me % 2
     my_t = me // 2
+    n_u = n_t // 2
+    side = my_t % 2
+    my_u = my_t // 2
     half = p % 2
     mate = p + 1 - 2 * half
     other = me + 1 - 2 * core
@@ -73,19 +80,19 @@
     for load in loads:
         load.start()
 
-    psum_buf[...] = jnp.zeros_like(psum_buf)
     barrier = pltpu.get_barrier_semaphore()
 
-    def greet_aux(s, _):
-        pl.semaphore_signal(barrier, inc=1, device_id=((me + s) % n_aux, p), device_id_type=MESH)
-        return 0
-
-    def greet_pair(s, _):
-        pl.semaphore_signal(barrier, inc=1, device_id=(me, (p + s) % n_pair), device_id_type=MESH)
-        return 0
-
-    lax.fori_loop(1, n_pair, greet_pair, 0)
-    lax.fori_loop(1, n_aux, greet_aux, 0)
+    def greet(s, _):
+        for q in range(n_pair):
+            @pl.when((s > 0) | (q > 0))
+            def _():
+                pl.semaphore_signal(
+                    barrier, inc=1, device_id=(wrap(me + s, n_aux), wrap(p + q, n_pair)),
+                    device_id_type=MESH,
+                )
+        return 0
+
+    lax.fori_loop(0, n_aux, greet, 0, unroll=8)
 
     held[count] = jnp.zeros(held.shape[1:], BF16)
     part[count] = jnp.zeros(part.shape[1:], F32)
@@ -97,7 +104,7 @@
     fill.wait()
     own = [held[tab_ref[4, i], :16, :].astype(F32)[:HALF] for i in range(4)]
     wsend[...] = jnp.concatenate(own, axis=0).astype(BF16)
-    pl.semaphore_wait(barrier, n_aux + n_pair - 2)
+    pl.semaphore_wait(barrier, n_aux * n_pair - 1)
     wcopy = pltpu.make_async_remote_copy(
         src_ref=wsend, dst_ref=wrecv, send_sem=w_sems.at[0], recv_sem=w_sems.at[1],
         device_id=(me, mate), device_id_type=MESH,
@@ -136,7 +143,7 @@
         )
         return 0
 
-    lax.fori_loop(0, count, contract, 0, unroll=4)
+    lax.fori_loop(0, count, contract, 0, unroll=32)
 
     def first_block(d):
         return (d * slab) // lanes
@@ -151,37 +158,67 @@
             device_id=(other, p), device_id_type=MESH,
         )
 
-    def d_copy(t, slot):
+    def x_copy(u):
         return pltpu.make_async_remote_copy(
-            src_ref=dsend.at[t], dst_ref=drecv.at[slot],
-            send_sem=ds_sems.at[t], recv_sem=dr_sems.at[slot],
-            device_id=(2 * t + core, p), device_id_type=MESH,
-        )
-
-    def to_core(s, _):
-        t = (my_t + s) % n_t
-        d = 2 * t + 1 - core
-        for c in range(2):
-            for j in range(nb):
-                csend[t, 16 * c : 16 * (c + 1), lanes * j : lanes * (j + 1)] = piece(d, c, j)
-        c_copy(t).start()
-        return 0
-
-    lax.fori_loop(1, n_t + 1, to_core, 0)
-
-    def to_chip(s, _):
-        t = (my_t + s) % n_t
-        d = 2 * t + core
+            src_ref=xsend.at[u], dst_ref=xrecv.at[u],
+            send_sem=xs_sems.at[u], recv_sem=xr_sems.at[u],
+            device_id=(2 * (my_t + 1 - 2 * side) + core, p), device_id_type=MESH,
+        )
+
+    def z_copy(u, slot):
+        return pltpu.make_async_remote_copy(
+            src_ref=zsend.at[u], dst_ref=zrecv.at[slot],
+            send_sem=zs_sems.at[u], recv_sem=zr_sems.at[slot],
+            device_id=(2 * (2 * u + side) + core, p), device_id_type=MESH,
+        )
+
+    def turn(i):
+        split = n_u - n_u // 2
+        step = jnp.where(i < split, n_u // 2 + i, i - split + 1)
+        return wrap(my_u + jnp.where(i == n_u - 1, 0, step), n_u)
+
+    tiles = [
+        (c, j, (slice(16 * c, 16 * (c + 1)), slice(lanes * j, lanes * (j + 1))))
+        for c in range(2)
+        for j in range(nb)
+    ]
+
+    def to_core(i, _):
+        u = turn(i)
+        for b in (1 - side, side):
+            t = 2 * u + b
+            for c, j, here in tiles:
+                csend[(t,) + here] = piece(2 * t + 1 - core, c, j)
+            c_copy(t).start()
+        return 0
+
+    lax.fori_loop(0, n_u, to_core, 0)
+
+    def to_side(i, _):
+        u = turn(i)
+        t = 2 * u + 1 - side
         c_copy(t).wait_recv()
-        for c in range(2):
-            for j in range(nb):
-                here = (slice(16 * c, 16 * (c + 1)), slice(lanes * j, lanes * (j + 1)))
-                dsend[(t,) + here] = (piece(d, c, j) + crecv[(t,) + here]).astype(BF16)
-        d_copy(t, my_t).start()
-        return 0
-
-    lax.fori_loop(1, n_t, to_chip, 0)
-    c_copy(my_t).wait_recv()
+        for c, j, here in tiles:
+            xsend[(u,) + here] = (piece(2 * t + core, c, j) + crecv[(t,) + here]).astype(BF16)
+        x_copy(u).start()
+        return 0
+
+    lax.fori_loop(0, n_u, to_side, 0)
+
+    def merged(u, c, j, here):
+        t = 2 * u + side
+        return piece(2 * t + core, c, j) + crecv[(t,) + here] + xrecv[(u,) + here].astype(F32)
+
+    def to_line(i, _):
+        u = turn(i)
+        c_copy(2 * u + side).wait_recv()
+        x_copy(u).wait_recv()
+        for c, j, here in tiles:
+            zsend[(u,) + here] = merged(u, c, j, here).astype(BF16)
+        z_copy(u, my_u).start()
+        return 0
+
+    lax.fori_loop(0, n_u - 1, to_line, 0)
 
     for load in loads[3:]:
         load.wait()
@@ -194,27 +231,19 @@
     tops = jnp.where(sub < HALF, ven_ref[0:1, :], ven_ref[nvb : nvb + 1, :])
     column = jnp.sum(jnp.where(lane == sub % HALF, tops, 0.0), axis=1, keepdims=True)
 
-    totals = []
-    for c in range(2):
-        for j in range(nb):
-            here = (slice(16 * c, 16 * (c + 1)), slice(lanes * j, lanes * (j + 1)))
-            totals.append(piece(me, c, j) + crecv[(my_t,) + here])
+    c_copy(my_t).wait_recv()
+    x_copy(my_u).wait_recv()
+    totals = [merged(my_u, c, j, here) for c, j, here in tiles]
 
     def arrive(s, totals):
-        t = (my_t + n_t - s) % n_t
-        pltpu.make_async_remote_copy(
-            src_ref=dsend.at[t], dst_ref=drecv.at[t],
-            send_sem=ds_sems.at[t], recv_sem=dr_sems.at[t],
-            device_id=(2 * t + core, p), device_id_type=MESH,
-        ).wait_recv()
-        out = []
-        for c in range(2):
-            for j in range(nb):
-                here = (slice(16 * c, 16 * (c + 1)), slice(lanes * j, lanes * (j + 1)))
-                out.append(totals[c * nb + j] + drecv[(t,) + here].astype(F32))
-        return tuple(out)
-
-    totals = lax.fori_loop(1, n_t, arrive, tuple(totals))
+        u = wrap(my_u + s, n_u)
+        z_copy(u, u).wait_recv()
+        return tuple(
+            total + zrecv[(u,) + here].astype(F32)
+            for total, (_, _, here) in zip(totals, tiles)
+        )
+
+    totals = lax.fori_loop(1, n_u, arrive, tuple(totals))
 
     grams = [[jnp.zeros((HALF, HALF), F32) for _ in range(2)] for _ in range(2)]
     for j in range(nb):
@@ -236,65 +265,37 @@
                 grams[a][b] += lax.dot_general(
                     heads[a], tails[b], (((1,), (1,)), ((), ())), preferred_element_type=F32
                 )
-    psum_buf[p, :, :HALF] = (
-        2.0 * (grams[0][0] + grams[1][1]) - grams[1][0] - grams[0][1]
-    )
-
-    def p_copy(q, slot):
-        return pltpu.make_async_remote_copy(
-            src_ref=psum_buf.at[p], dst_ref=psum_buf.at[slot],
-            send_sem=ps_sems.at[q], recv_sem=pr_sems.at[slot],
-            device_id=(me, q), device_id_type=MESH,
-        )
-
-    def p_send(s, _):
-        p_copy((p + s) % n_pair, p).start()
-        return 0
-
-    lax.fori_loop(1, n_pair, p_send, 0)
-
-    def p_wait(s, _):
-        q = (p + s) % n_pair
-        p_copy(q, q).wait()
-        return 0
-
-    lax.fori_loop(1, n_pair, p_wait, 0)
-    total = psum_buf[0]
-    for q in range(1, n_pair):
-        total = total + psum_buf[q]
-    asum_buf[me] = total
-
-    def a_copy(d, slot):
-        return pltpu.make_async_remote_copy(
-            src_ref=asum_buf.at[me], dst_ref=asum_buf.at[slot],
-            send_sem=as_sems.at[d], recv_sem=ar_sems.at[slot],
-            device_id=(d, p), device_id_type=MESH,
-        )
-
-    def a_send(s, _):
-        a_copy((me + s) % n_aux, me).start()
-        return 0
-
-    lax.fori_loop(1, n_aux, a_send, 0)
-
-    def sent(s, _):
-        t = (my_t + s) % n_t
-        d_copy(t, my_t).wait_send()
-        c_copy(t).wait_send()
-        return 0
-
-    lax.fori_loop(1, n_t, sent, 0)
-    c_copy(my_t).wait_send()
-
-    def a_wait(s, _):
-        d = (me + s) % n_aux
-        a_copy(d, d).wait()
-        return 0
-
-    lax.fori_loop(1, n_aux, a_wait, 0)
-    total = asum_buf[0]
-    for d in range(1, n_aux):
-        total = total + asum_buf[d]
+    mine = me * n_pair + p
+    sums[mine] = jnp.zeros(sums.shape[1:], F32)
+    sums[mine, :, :HALF] = 2.0 * (grams[0][0] + grams[1][1]) - grams[1][0] - grams[0][1]
+
+    def share(s, _):
+        for q in range(n_pair):
+            @pl.when((s > 0) | (q > 0))
+            def _():
+                pltpu.make_async_remote_copy(
+                    src_ref=sums.at[mine], dst_ref=sums.at[mine],
+                    send_sem=sum_sems.at[0], recv_sem=sum_sems.at[1],
+                    device_id=(wrap(me + s, n_aux), wrap(p + q, n_pair)), device_id_type=MESH,
+                ).start()
+        return 0
+
+    lax.fori_loop(0, n_aux, share, 0, unroll=8)
+
+    def sent(u, _):
+        c_copy(2 * u).wait_send()
+        c_copy(2 * u + 1).wait_send()
+        x_copy(u).wait_send()
+        pl.when(u != my_u)(lambda: z_copy(u, my_u).wait_send())
+        return 0
+
+    lax.fori_loop(0, n_u, sent, 0)
+    peers = sums.at[pl.ds(0, n_aux * n_pair - 1)]
+    pltpu.make_async_copy(peers, peers, sum_sems.at[0]).wait()
+    pltpu.make_async_copy(peers, peers, sum_sems.at[1]).wait()
+    total = sums[0]
+    for d in range(1, n_aux * n_pair):
+        total = total + sums[d]
     den_ref[...] = (total / math.sqrt(V))[:, :HALF]
 
 
@@ -310,6 +311,7 @@
     nb = max(-(-((d + 1) * slab) // lanes) - d * slab // lanes for d in range(n_aux))
     shard = metric.shape[1]
     n_t = n_aux // 2
+    n_u = n_t // 2
     vmem = pl.BlockSpec(memory_space=pltpu.VMEM)
     hbm = pl.BlockSpec(memory_space=pltpu.HBM)
     dma = pltpu.SemaphoreType.DMA
@@ -336,20 +338,20 @@
             pltpu.VMEM((32, lanes), BF16),
             pltpu.VMEM((n_t, 32, nb * lanes), F32),
             pltpu.VMEM((n_t, 32, nb * lanes), F32),
-            pltpu.VMEM((n_t, 32, nb * lanes), BF16),
-            pltpu.VMEM((n_t, 32, nb * lanes), BF16),
-            pltpu.VMEM((n_pair, HALF, lanes), F32),
-            pltpu.VMEM((n_aux, HALF, lanes), F32),
+            pltpu.VMEM((n_u, 32, nb * lanes), BF16),
+            pltpu.VMEM((n_u, 32, nb * lanes), BF16),
+            pltpu.VMEM((n_u, 32, nb * lanes), BF16),
+            pltpu.VMEM((n_u, 32, nb * lanes), BF16),
+            pltpu.VMEM((n_aux * n_pair, HALF, lanes), F32),
             dma((7,)),
             dma((2,)),
             dma((n_t,)),
             dma((n_t,)),
-            dma((n_t,)),
-            dma((n_t,)),
-            dma((n_pair,)),
-            dma((n_pair,)),
-            dma((n_aux,)),
-            dma((n_aux,)),
+            dma((n_u,)),
+            dma((n_u,)),
+            dma((n_u,)),
+            dma((n_u,)),
+            dma((2,)),
         ],
         compiler_params=pltpu.CompilerParams(
             collective_id=0, has_side_effects=True, vmem_limit_bytes=60 * 2**20

time: 32.1 us -> 28.2 us (0.88)
  Pallas kernels: 29.3 us -> 25.3 us
    pallas_call x1, Pallas kernels: 29.3 us -> 25.3 us  [body(): pl.pallas_call(functools.partial(main_kernel, n_aux, n_pair, nvb, slab, n...]
where the time goes in v3:
time: 28.2 us; the launch traced here: 27.9 us
  Pallas kernels  25.3 us (90%)
  local copies, waits for them, and re-layouts  1.93 us (7%)
  between operations  0.65 us (2%)
    pallas_call x1, Pallas kernels, body(): pl.pallas_call(functools.partial(main_kernel, n_aux, n_pair, nvb, slab, n...  25.3 us
    unnamed x4, local copies, waits for them, and re-layouts  1.93 us

profile of v3, /device:TPU:0, one launch (start us, length us, event | category | flops | bytes accessed | tf_op | source)
XLA Modules:
  0.0 27.9 jit_solution(8310770421026100335)
XLA Ops:
  0.6 25.3 %amplitudes.1 = (bf16[16,640]{1,0:T(8,128)(2,1)}, f32[8,8]{1,0:T(8,128)}) custom-call(s32[3,1,32]{2,1,0:T(1,128)} %bitcast.9, f32[8000]{0:T(1024)} %occ_hbm.1, s32[1,2]{1,0:T(1,128)} %pair_hbm.1, bf16[32,128,128]{2,1,0:T(8,128)(2,1)} %bitcast.6, bf16[256,256]{1,0:T(8,128)(2,1)} %metric_hbm.1, f32[160,128]{1,0:T(8,128)} %bitcast.7), custom_call_target="tpu_custom_call" | custom-call | tf_op jit(solution)/shard_map/amplitudes/pallas_call | solution.py:318
  26.0 0.0 copy-start
  26.0 1.3 %copy.10 = bf16[1,16,640]{2,1,0:T(8,128)(2,1)} copy(bf16[1,16,640]{2,1,0:T(8,128)(2,1)} %bitcast.8) | data formatting | bytes 40960
  27.3 0.0 copy-done
  27.3 0.6 %copy.11 = f32[8,8]{1,0:T(8,128)} copy(f32[8,8]{1,0:T(8,128)S(1)} %copy-done) | data formatting | bytes 512
Async XLA Ops:
  26.0 1.3 %copy-start = (f32[8,8]{1,0:T(8,128)S(1)}, f32[8,8]{1,0:T(8,128)}, u32[]{:S(2)}) copy-start(f32[8,8]{1,0:T(8,128)} %get-tuple-element.9) | copy-start | bytes 772

commit v4 on v3

--- a/solution.py
+++ b/solution.py
@@ -80,19 +80,23 @@
     for load in loads:
         load.start()
 
+    sums[me * n_pair + p] = jnp.zeros(sums.shape[1:], F32)
     barrier = pltpu.get_barrier_semaphore()
 
-    def greet(s, _):
+    def greet(s, q):
+        pl.semaphore_signal(
+            barrier, inc=1, device_id=(wrap(me + s, n_aux), wrap(p + q, n_pair)),
+            device_id_type=MESH,
+        )
+
+    def greet_all(s, _):
         for q in range(n_pair):
-            @pl.when((s > 0) | (q > 0))
-            def _():
-                pl.semaphore_signal(
-                    barrier, inc=1, device_id=(wrap(me + s, n_aux), wrap(p + q, n_pair)),
-                    device_id_type=MESH,
-                )
-        return 0
-
-    lax.fori_loop(0, n_aux, greet, 0, unroll=8)
+            greet(s, q)
+        return 0
+
+    for q in range(1, n_pair):
+        greet(0, q)
+    lax.fori_loop(1, n_aux, greet_all, 0, unroll=5)
 
     held[count] = jnp.zeros(held.shape[1:], BF16)
     part[count] = jnp.zeros(part.shape[1:], F32)
@@ -266,21 +270,23 @@
                     heads[a], tails[b], (((1,), (1,)), ((), ())), preferred_element_type=F32
                 )
     mine = me * n_pair + p
-    sums[mine] = jnp.zeros(sums.shape[1:], F32)
     sums[mine, :, :HALF] = 2.0 * (grams[0][0] + grams[1][1]) - grams[1][0] - grams[0][1]
 
-    def share(s, _):
+    def share(s, q):
+        pltpu.make_async_remote_copy(
+            src_ref=sums.at[mine], dst_ref=sums.at[mine],
+            send_sem=sum_sems.at[0], recv_sem=sum_sems.at[1],
+            device_id=(wrap(me + s, n_aux), wrap(p + q, n_pair)), device_id_type=MESH,
+        ).start()
+
+    def share_all(s, _):
         for q in range(n_pair):
-            @pl.when((s > 0) | (q > 0))
-            def _():
-                pltpu.make_async_remote_copy(
-                    src_ref=sums.at[mine], dst_ref=sums.at[mine],
-                    send_sem=sum_sems.at[0], recv_sem=sum_sems.at[1],
-                    device_id=(wrap(me + s, n_aux), wrap(p + q, n_pair)), device_id_type=MESH,
-                ).start()
-        return 0
-
-    lax.fori_loop(0, n_aux, share, 0, unroll=8)
+            share(s, q)
+        return 0
+
+    lax.fori_loop(1, n_aux, share_all, 0, unroll=5)
+    for q in range(1, n_pair):
+        share(0, q)
 
     def sent(u, _):
         c_copy(2 * u).wait_send()

time: 28.2 us -> 28.1 us (level)
  no operation moved by 1% of the time
where the time goes in v4:
time: 28.1 us; the launch traced here: 27.9 us
  Pallas kernels  25.3 us (90%)
  local copies, waits for them, and re-layouts  1.93 us (7%)
  between operations  0.65 us (2%)
    pallas_call x1, Pallas kernels, body(): pl.pallas_call(functools.partial(main_kernel, n_aux, n_pair, nvb, slab, n...  25.3 us
    unnamed x4, local copies, waits for them, and re-layouts  1.93 us

profile of v4, /device:TPU:0, one launch (start us, length us, event | category | flops | bytes accessed | tf_op | source)
XLA Modules:
  0.0 27.9 jit_solution(18173541730331744383)
XLA Ops:
  0.6 25.3 %amplitudes.1 = (bf16[16,640]{1,0:T(8,128)(2,1)}, f32[8,8]{1,0:T(8,128)}) custom-call(s32[3,1,32]{2,1,0:T(1,128)} %bitcast.9, f32[8000]{0:T(1024)} %occ_hbm.1, s32[1,2]{1,0:T(1,128)} %pair_hbm.1, bf16[32,128,128]{2,1,0:T(8,128)(2,1)} %bitcast.6, bf16[256,256]{1,0:T(8,128)(2,1)} %metric_hbm.1, f32[160,128]{1,0:T(8,128)} %bitcast.7), custom_call_target="tpu_custom_call" | custom-call | tf_op jit(solution)/shard_map/amplitudes/pallas_call | solution.py:324
  26.0 0.0 copy-start
  26.0 1.3 %copy.10 = bf16[1,16,640]{2,1,0:T(8,128)(2,1)} copy(bf16[1,16,640]{2,1,0:T(8,128)(2,1)} %bitcast.8) | data formatting | bytes 40960
  27.3 0.0 copy-done
  27.3 0.6 %copy.11 = f32[8,8]{1,0:T(8,128)} copy(f32[8,8]{1,0:T(8,128)S(1)} %copy-done) | data formatting | bytes 512
Async XLA Ops:
  26.0 1.3 %copy-start = (f32[8,8]{1,0:T(8,128)S(1)}, f32[8,8]{1,0:T(8,128)}, u32[]{:S(2)}) copy-start(f32[8,8]{1,0:T(8,128)} %get-tuple-element.9) | copy-start | bytes 772
